TPU v7x, 256 devices: a whole 4x4x8 slice. The times are simulated.
256 devices in a mesh: cont: 8 (over z), line: 8 (over y, core), scen: 4 (over x).
Axes of the slice: x: 4, y: 4, z: 8, core: 2. Of those that a mesh axis runs over, the one named last changes fastest.
Arguments:
- lodf: bfloat16 [1024, 4096], P('line', 'cont'), may hold values from -1 to 1
- flow: float32 [1024, 256], P('line', 'scen'), may hold values from -6 to 6
- out_flow: float32 [256, 4096], P('scen', 'cont'), may hold values from -6 to 6
- limits: float32 [1024], P('line'), may hold values from 0.5 to 2
- ptdf_mon: bfloat16 [1024, 2048], P('line'), may hold values from -6 to 6
- ptdf_out: bfloat16 [4096, 2048], P('cont'), may hold values from -6 to 6
- viol_cont: int32 [131072], P(('cont', 'line', 'scen')), may hold values from 0 to 511
- viol_line: int32 [131072], P(('cont', 'line', 'scen')), may hold values from 0 to 127
- viol_scen: int32 [131072], P(('cont', 'line', 'scen')), may hold values from 0 to 63
- rows_used: int32 [256], P(('cont', 'line', 'scen')), may hold values from 64 to 512, as said below
Outputs:
- worst: float32 [1024, 256], P('line', 'scen')
- schur: float32 [2048, 2048], P(('line', 'scen'))
Inputs may be any that keep to these rules, and one draw needn't show every extreme that they name: `rows_used`: each device uses a leading run of its 512 slots; the counts are skewed, and some device is full.
All inputs are finite; a program needn't handle non-finite values.
Results may differ from a plain program's by a relative error of at most 0.00096.
Values may be sent and summed in bfloat16 or wider, within the bound.
No kernel may reach another device: no remote copies, remote signals or barrier semaphores. Data moves between devices by JAX's collectives and lax.ppermute only.
A program may use at most 128 MiB of HBM per device.

v0:
```python
import math
import jax
import jax.numpy as jnp
from jax import lax
from jax.sharding import PartitionSpec as P


def local(
    lodf, flow, out_flow, limits, ptdf_mon, ptdf_out, viol_cont, viol_line, viol_scen, rows_used
):
    line_dev, cont_dev = lodf.shape
    scen_dev = flow.shape[1]
    width = ptdf_mon.shape[1]
    n_rows = viol_cont.shape[0]
    n_cont = lax.axis_size("cont")
    n_line = lax.axis_size("line")
    n_scen = lax.axis_size("scen")
    owners = n_line * n_scen
    devices = n_cont * owners
    row_block = math.gcd(n_rows, 512)
    lines_each = math.gcd(line_dev, 32)

    def screen(pair):
        lodf_block, flow_block = pair
        post = (
            flow_block[:, :, None]
            + lodf_block.astype(jnp.float32)[:, None, :] * out_flow[None, :, :]
        )
        return jnp.max(jnp.abs(post), axis=2)

    local_worst = lax.map(
        screen,
        (
            lodf.reshape(line_dev // lines_each, lines_each, cont_dev),
            flow.reshape(line_dev // lines_each, lines_each, scen_dev),
        ),
    ).reshape(line_dev, scen_dev)
    worst = lax.pmax(local_worst, "cont") / limits[:, None]
    coef = lodf[viol_line, viol_cont].astype(jnp.float32)
    rows = (
        ptdf_mon[viol_line].astype(jnp.float32)
        + coef[:, None] * ptdf_out[viol_cont].astype(jnp.float32)
    ).astype(jnp.bfloat16)
    rows = lax.optimization_barrier(rows)
    post = flow[viol_line, viol_scen] + coef * out_flow[viol_scen, viol_cont]
    ratio = post / limits[viol_line]
    live = jnp.arange(n_rows, dtype=jnp.int32) < rows_used[0]
    weight = jnp.where(live, 1.0 + ratio * ratio, jnp.zeros_like(ratio))
    scaled = (weight[:, None] * rows.astype(jnp.float32)).astype(jnp.bfloat16)
    trips = (rows_used[0] + row_block - 1) // row_block
    row_blocks = rows.reshape(n_rows // row_block, row_block, width)
    scaled_blocks = scaled.reshape(n_rows // row_block, row_block, width)

    def step(index, acc):
        row_tile = lax.dynamic_index_in_dim(row_blocks, index, 0, keepdims=False)
        scaled_tile = lax.dynamic_index_in_dim(scaled_blocks, index, 0, keepdims=False)
        return acc + lax.dot_general(
            row_tile, scaled_tile, (((0,), (0,)), ((), ())), preferred_element_type=jnp.float32
        )

    owned = lax.psum_scatter(
        lax.fori_loop(
            0,
            trips,
            step,
            jnp.zeros((lax.axis_size(("line", "scen")) * (width // owners), width), jnp.float32),
        ),
        ("line", "scen"),
        scatter_dimension=0,
        tiled=True,
    )
    total = lax.psum(owned, "cont")
    schur = total * (1.0 / (n_rows * devices))
    return (worst, schur)


def solution(mesh):
    in_specs = (
        P("line", "cont"),
        P("line", "scen"),
        P("scen", "cont"),
        P("line"),
        P("line", None),
        P("cont", None),
        P(("cont", "line", "scen")),
        P(("cont", "line", "scen")),
        P(("cont", "line", "scen")),
        P(("cont", "line", "scen")),
    )
    out_specs = (P("line", "scen"), P(("line", "scen"), None))
    return jax.shard_map(local, mesh=mesh, in_specs=in_specs, out_specs=out_specs, check_vma=False)
```

profile of v0, /device:TPU:2, one launch (start us, length us, event | category | flops | bytes accessed | tf_op | source)
XLA Modules:
  0.0 275.0 jit_solution(17831814919024099587)
XLA Ops:
  7.2 0.0 reduce-scatter.2.cloned.1.call-start
  8.1 0.7 shift-left_or_fusion
  8.8 5.2 %gather_fusion.1 = bf16[512]{0:T(512)(128)(2,1)S(1)} fusion(bf16[128,512]{1,0:T(8,128)(2,1)} %param.14, s32[512]{0:T(512)S(1)} %get-tuple-element.84), kind=kCustom, calls=%fused_computation.1 | custom fusion | bytes 6144 | tf_op jit(solution)/shard_map/gather | solution.py:39
  14.0 3.3 %gather_fusion = bf16[512,2048]{1,0:T(8,128)(2,1)} fusion(bf16[128,2048]{1,0:T(8,128)(2,1)S(1)} %copy-done.2, s32[1024]{0:T(1024)S(1)} %get-tuple-element.89), kind=kCustom, calls=%fused_computation | custom fusion | bytes 4196352 | tf_op jit(solution)/shard_map/gather | solution.py:41
  17.3 3.3 %gather_fusion.2 = bf16[512,2048]{1,0:T(8,128)(2,1)} fusion(bf16[512,2048]{1,0:T(8,128)(2,1)S(1)} %copy-done, s32[1024]{0:T(1024)S(1)} %get-tuple-element.88), kind=kCustom, calls=%fused_computation.2 | custom fusion | bytes 4196352 | tf_op jit(solution)/shard_map/gather | solution.py:42
  20.6 4.2 %add_convert_fusion = bf16[512,2048]{1,0:T(8,128)(2,1)} fusion(bf16[512,2048]{1,0:T(8,128)(2,1)} %gather_fusion.2, bf16[512,2048]{1,0:T(8,128)(2,1)} %gather_fusion, f32[512]{0:T(512)S(1)} %convert_element_type.36), kind=kLoop, calls=%fused_computation.14 | loop fusion | flops 5242880 | bytes 6293504 | tf_op jit(solution)/shard_map/convert_element_type | solution.py:43
  24.8 3.3 %gather_fusion.5 = f32[512]{0:T(512)S(1)} fusion(f32[128]{0:T(128)S(1)} %copy-done.1, s32[1024]{0:T(1024)S(1)} %get-tuple-element.89), kind=kCustom, calls=%fused_computation.5 | custom fusion | bytes 6144 | tf_op jit(solution)/shard_map/gather | solution.py:46
  28.2 3.7 %gather_fusion.3 = f32[512]{0:T(512)S(1)} fusion(f32[128,64]{0,1:T(8,128)S(1)} %copy-done.3, s32[512]{0:T(512)S(1)} %get-tuple-element.85), kind=kCustom, calls=%fused_computation.3 | custom fusion | bytes 8192 | tf_op jit(solution)/shard_map/gather | solution.py:45
  32.0 4.5 %gather_fusion.4 = f32[512]{0:T(512)S(1)} fusion(f32[64,512]{1,0:T(8,128)S(1)} %copy-done.4, s32[512]{0:T(512)S(1)} %get-tuple-element.83), kind=kCustom, calls=%fused_computation.4 | custom fusion | bytes 8192 | tf_op jit(solution)/shard_map/gather | solution.py:45
  36.5 3.3 %fusion.2 = bf16[1,512,2048]{2,1,0:T(8,128)(2,1)} fusion(bf16[512,2048]{1,0:T(8,128)(2,1)} %add_convert_fusion, f32[512]{0:T(512)S(1)} %add_select_fusion), kind=kLoop, calls=%fused_computation.15 | loop fusion | flops 3145728 | bytes 4196352 | tf_op jit(solution)/shard_map/reshape | solution.py:52
  39.8 7.9 %broadcast_in_dim.20 = f32[2048,2048]{1,0:T(8,128)} broadcast(f32[]{:T(128)} %constant.46.clone.1), dimensions={} | broadcast | bytes 16777220 | tf_op jit(solution)/shard_map/broadcast_in_dim | solution.py:66
  47.7 17.3 %while.21 = (s32[]{:T(128)}, f32[2048,2048]{1,0:T(8,128)}, s32[]{:T(128)}, bf16[1,512,2048]{2,1,0:T(8,128)(2,1)}, bf16[1,512,2048]{2,1,0:T(8,128)(2,1)}, /*index=5*/s32[]{:T(128)}) while((s32[]{:T(128)}, f32[2048,2048]{1,0:T(8,128)}, s32[]{:T(128)}, bf16[1,512,2048]{2,1,0:T(8,128)(2,1)}, bf16[1,512,2048]{2,1,0:T(8,128)(2,1)}, ...), condition=%wide.region_5.6_spmd, body=%wide.region_4.5_spmd.sunk | while | flops 4299161600 | bytes 37748804 | solution.py:62
  47.7 17.3 %convolution_add_fusion.2 = f32[2048,2048]{1,0:T(8,128)} fusion(f32[2048,2048]{1,0:T(8,128)} %get-tuple-element.178, bf16[1,512,2048]{2,1,0:T(8,128)(2,1)} %get-tuple-element.187, bf16[1,512,2048]{2,1,0:T(8,128)(2,1)} %get-tuple-element.186), kind=kOutput, calls=%fused_computation.10.clone.1 | convolution fusion | flops 4299161600 | bytes 37748736 | tf_op jit(solution)/shard_map/while/body/dot_general | solution.py:57
  65.1 0.0 reduce-scatter.2.cloned.1.call-update
  65.1 0.0 all-reduce.2.cloned.1.call-start
  65.1 0.1 copy.16
  65.2 125.7 %reduce-scatter.2.cloned.1.call-done = f32[64,2048]{1,0:T(8,128)} async-done(((f32[2048,2048]{1,0:T(8,128)}), f32[64,2048]{1,0:T(8,128)}) %reduce-scatter.2.cloned.1.call-update) | async-done | bytes 524304 | tf_op jit(solution)/shard_map/reduce_scatter | solution.py:61
  191.0 0.0 all-reduce.2.cloned.1.call-update
  191.0 7.2 %while.20 = (s32[]{:T(128)}, f32[4,32,64]{2,1,0:T(8,128)S(1)}, f32[4,32,64]{2,1,0:T(8,128)S(1)}, bf16[4,32,512]{2,1,0:T(8,128)(2,1)}, f32[64,512]{1,0:T(8,128)S(1)}, /*index=5*/s32[]{:T(128)}) while((s32[]{:T(128)}, f32[4,32,64]{2,1,0:T(8,128)S(1)}, f32[4,32,64]{2,1,0:T(8,128)S(1)}, bf16[4,32,512]{2,1,0:T(8,128)(2,1)}, ...), condition=%wide.region_2.3_spmd, body=%wide.region_0.2_spmd.sunk | while | flops 4208642 | bytes 360529 | solution.py:31
  191.0 0.8 bitcast_convert_fusion.2
  191.8 1.0 abs_reduce_fusion.2
  192.8 0.8 bitcast_convert_fusion.2
  193.6 1.0 abs_reduce_fusion.2
  194.6 0.8 bitcast_convert_fusion.2
  195.4 1.0 abs_reduce_fusion.2
  196.4 0.8 bitcast_convert_fusion.2
  197.2 1.0 abs_reduce_fusion.2
  198.2 30.7 %pmax.7 = f32[128,64]{1,0:T(8,128)S(1)} all-reduce(f32[128,64]{1,0:T(8,128)S(1)} %bitcast.35), channel_id=1, replica_groups=mesh['cont'=8,'line'=8,'scen'=4] {'cont'}, use_global_device_ids=true, to_apply=%region_3.4 | all-reduce | flops 8192 | bytes 65536 | tf_op jit(solution)/shard_map/pmax | solution.py:38
  228.9 0.1 broadcast_divide_fusion
  229.0 0.7 copy.17
  229.7 36.6 %all-reduce.2.cloned.1.call-done = f32[64,2048]{1,0:T(8,128)} async-done(((f32[64,2048]{1,0:T(8,128)}), f32[64,2048]{1,0:T(8,128)}) %all-reduce.2.cloned.1.call-update) | async-done | bytes 524304 | tf_op jit(solution)/shard_map/psum | solution.py:72
  266.3 1.9 broadcast_multiply_fusion
  (22 shorter events, 0.1 us)
Async XLA Ops:
  7.2 10.1 %copy-start = (bf16[512,2048]{1,0:T(8,128)(2,1)S(1)}, bf16[512,2048]{1,0:T(8,128)(2,1)}, u32[]{:S(2)}) copy-start(bf16[512,2048]{1,0:T(8,128)(2,1)} %param.19) | copy-start | bytes 6291460
  7.2 6.8 %copy-start.2 = (bf16[128,2048]{1,0:T(8,128)(2,1)S(1)}, bf16[128,2048]{1,0:T(8,128)(2,1)}, u32[]{:S(2)}) copy-start(bf16[128,2048]{1,0:T(8,128)(2,1)} %param.18) | copy-start | bytes 1572868
  7.2 183.8 %reduce-scatter.2.cloned.1.call-start = ((), (), s32[]{:S(2)}) async-start(), calls=%async_computation.1 | async-start | bytes 17301504 | tf_op jit(solution)/shard_map/reduce_scatter | solution.py:61
  20.6 4.2 %copy-start.1 = (f32[128]{0:T(128)S(1)}, f32[128]{0:T(128)}, u32[]{:S(2)}) copy-start(f32[128]{0:T(128)} %param.17) | copy-start | bytes 1540
  24.8 3.4 %copy-start.3 = (f32[128,64]{0,1:T(8,128)S(1)}, f32[128,64]{0,1:T(8,128)}, u32[]{:S(2)}) copy-start(f32[128,64]{0,1:T(8,128)} %param.15) | copy-start | bytes 98308
  24.8 7.1 %copy-start.4 = (f32[64,512]{1,0:T(8,128)S(1)}, f32[64,512]{1,0:T(8,128)}, u32[]{:S(2)}) copy-start(f32[64,512]{1,0:T(8,128)} %param.16) | copy-start | bytes 393220
  65.1 201.2 %all-reduce.2.cloned.1.call-start = ((), (), s32[]{:S(2)}) async-start(), calls=%async_computation.2 | async-start | bytes 1048576 | tf_op jit(solution)/shard_map/psum | solution.py:72
Sparse Core Ops, SparseCore 0:
  65.2 125.7 reduce-scatter.1
  193.3 72.9 all-reduce.1
where the time goes:
time: 276 us; the launch traced here: 275 us
  waiting for transfers between devices  162 us (59%)
  local copies, waits for them, and re-layouts  32.1 us (12%)
  blocking collectives  30.7 us (11%)
  other arithmetic  17.3 us (6%)
  matrix products  17.3 us (6%)
  between operations  15 us (5%)
    reduce_scatter x1, waiting for transfers between devices, local(): lax.psum_scatter(lax.fori_loop(0, trips, step, jnp.zeros((lax.axis_size((...  126 us
    psum x1, waiting for transfers between devices, local(): total = lax.psum(owned, 'cont')  36.6 us
    pmax x1, blocking collectives, local(): worst = lax.pmax(local_worst, 'cont') / limits[:, None]  30.7 us
    dot_general x1, matrix products, step(): lax.dot_general(row_tile, scaled_tile, (((0,), (0,)), ((), ())), preferre...  17.3 us
    gather x2, local copies, waits for them, and re-layouts, local(): post = flow[viol_line, viol_scen] + coef * out_flow[viol_scen, viol_cont]  8.27 us
    broadcast_in_dim x1, local copies, waits for them, and re-layouts, local(): jnp.zeros((lax.axis_size(('line', 'scen')) * (width // owners), width), j...  7.86 us
  transfers between devices with their start and end apart: 2, of which 2 were waited for; matrix products, arithmetic and copies ran while one was open for 3% of the time, Pallas kernels for 0%

commit v1 on v0

--- a/solution.py
+++ b/solution.py
@@ -3,6 +3,7 @@
 import jax.numpy as jnp
 from jax import lax
 from jax.sharding import PartitionSpec as P
+from jax.lax import axis_size, ppermute
 
 
 def local(
@@ -69,7 +70,22 @@
         scatter_dimension=0,
         tiled=True,
     )
-    total = lax.psum(owned, "cont")
+
+    def _press_slot(across, here_x):
+        num = axis_size(across)
+
+        def check_tables_now(reply, tmp):
+            if tmp >= num:
+                return reply
+            return check_tables_now(
+                reply
+                + ppermute(reply, axis_name=across, perm=[(nth, nth ^ tmp) for nth in range(num)]),
+                2 * tmp,
+            )
+
+        return check_tables_now(here_x, 1)
+
+    total = _press_slot("cont", owned)
     schur = total * (1.0 / (n_rows * devices))
     return (worst, schur)
 

time: 276 us -> 290 us (1.051)
  starting transfers between devices: 0.08 us -> 10.2 us
  blocking collectives: 30.7 us -> 37.9 us
  waiting for transfers between devices: 162 us -> 158 us
    psum x1 -> x0, waiting for transfers between devices: 36.6 us -> none  [local(): total = lax.psum(owned, 'cont')]
    ppermute x0 -> x3, waiting for transfers between devices: none -> 32.3 us  [check_tables_now(): ppermute(reply, axis_name=across, perm=[(nth, nth ^ tmp) for nth in range...]
    ppermute x0 -> x3, starting transfers between devices: none -> 10.1 us  [check_tables_now(): ppermute(reply, axis_name=across, perm=[(nth, nth ^ tmp) for nth in range...]
    pmax x1, blocking collectives: 30.7 us -> 37.9 us  [local(): worst = lax.pmax(local_worst, 'cont') / limits[:, None]]
  transfers between devices with their start and end apart: 2 -> 4, of which waited for: 2 -> 3; matrix products, arithmetic and copies ran while one was open for 3% -> 3% of each run, Pallas kernels for 0% -> 0%
where the time goes in v1:
time: 290 us; the launch traced here: 289 us
  waiting for transfers between devices  158 us (54%)
  blocking collectives  37.9 us (13%)
  local copies, waits for them, and re-layouts  32.1 us (11%)
  other arithmetic  18.5 us (6%)
  matrix products  17.3 us (6%)
  between operations  15 us (5%)
  starting transfers between devices  10.2 us (4%)
    reduce_scatter x1, waiting for transfers between devices, local(): lax.psum_scatter(lax.fori_loop(0, trips, step, jnp.zeros((lax.axis_size((...  126 us
    pmax x1, blocking collectives, local(): worst = lax.pmax(local_worst, 'cont') / limits[:, None]  37.9 us
    ppermute x3, waiting for transfers between devices, check_tables_now(): ppermute(reply, axis_name=across, perm=[(nth, nth ^ tmp) for nth in range...  32.3 us
    dot_general x1, matrix products, step(): lax.dot_general(row_tile, scaled_tile, (((0,), (0,)), ((), ())), preferre...  17.3 us
    ppermute x3, starting transfers between devices, check_tables_now(): ppermute(reply, axis_name=across, perm=[(nth, nth ^ tmp) for nth in range...  10.1 us
    gather x2, local copies, waits for them, and re-layouts, local(): post = flow[viol_line, viol_scen] + coef * out_flow[viol_scen, viol_cont]  8.27 us
    broadcast_in_dim x1, local copies, waits for them, and re-layouts, local(): jnp.zeros((lax.axis_size(('line', 'scen')) * (width // owners), width), j...  7.86 us
  transfers between devices with their start and end apart: 4, of which 3 were waited for; matrix products, arithmetic and copies ran while one was open for 3% of the time, Pallas kernels for 0%

profile of v1, /device:TPU:2, one launch (start us, length us, event | category | flops | bytes accessed | tf_op | source)
XLA Modules:
  0.0 289.3 jit_solution(11037322101690842595)
XLA Ops:
  8.1 0.7 shift-left_or_fusion
  8.8 5.2 %gather_fusion.1 = bf16[512]{0:T(512)(128)(2,1)S(1)} fusion(bf16[128,512]{1,0:T(8,128)(2,1)} %param.14, s32[512]{0:T(512)S(1)} %get-tuple-element.84), kind=kCustom, calls=%fused_computation.1 | custom fusion | bytes 6144 | tf_op jit(solution)/shard_map/gather | solution.py:40
  14.0 3.4 %gather_fusion = bf16[512,2048]{1,0:T(8,128)(2,1)} fusion(bf16[128,2048]{1,0:T(8,128)(2,1)S(1)} %copy-done.2, s32[1024]{0:T(1024)S(1)} %get-tuple-element.89), kind=kCustom, calls=%fused_computation | custom fusion | bytes 4196352 | tf_op jit(solution)/shard_map/gather | solution.py:42
  17.3 3.3 %gather_fusion.2 = bf16[512,2048]{1,0:T(8,128)(2,1)} fusion(bf16[512,2048]{1,0:T(8,128)(2,1)S(1)} %copy-done, s32[1024]{0:T(1024)S(1)} %get-tuple-element.88), kind=kCustom, calls=%fused_computation.2 | custom fusion | bytes 4196352 | tf_op jit(solution)/shard_map/gather | solution.py:43
  20.6 4.2 %add_convert_fusion = bf16[512,2048]{1,0:T(8,128)(2,1)} fusion(bf16[512,2048]{1,0:T(8,128)(2,1)} %gather_fusion.2, bf16[512,2048]{1,0:T(8,128)(2,1)} %gather_fusion, f32[512]{0:T(512)S(1)} %convert_element_type.36), kind=kLoop, calls=%fused_computation.14 | loop fusion | flops 5242880 | bytes 6293504 | tf_op jit(solution)/shard_map/convert_element_type | solution.py:44
  24.9 3.3 %gather_fusion.5 = f32[512]{0:T(512)S(1)} fusion(f32[128]{0:T(128)S(1)} %copy-done.1, s32[1024]{0:T(1024)S(1)} %get-tuple-element.89), kind=kCustom, calls=%fused_computation.5 | custom fusion | bytes 6144 | tf_op jit(solution)/shard_map/gather | solution.py:47
  28.2 3.7 %gather_fusion.3 = f32[512]{0:T(512)S(1)} fusion(f32[128,64]{0,1:T(8,128)S(1)} %copy-done.3, s32[512]{0:T(512)S(1)} %get-tuple-element.85), kind=kCustom, calls=%fused_computation.3 | custom fusion | bytes 8192 | tf_op jit(solution)/shard_map/gather | solution.py:46
  32.0 4.5 %gather_fusion.4 = f32[512]{0:T(512)S(1)} fusion(f32[64,512]{1,0:T(8,128)S(1)} %copy-done.4, s32[512]{0:T(512)S(1)} %get-tuple-element.83), kind=kCustom, calls=%fused_computation.4 | custom fusion | bytes 8192 | tf_op jit(solution)/shard_map/gather | solution.py:46
  36.5 3.4 %fusion.2 = bf16[1,512,2048]{2,1,0:T(8,128)(2,1)} fusion(bf16[512,2048]{1,0:T(8,128)(2,1)} %add_convert_fusion, f32[512]{0:T(512)S(1)} %add_select_fusion), kind=kLoop, calls=%fused_computation.15 | loop fusion | flops 3145728 | bytes 4196352 | tf_op jit(solution)/shard_map/reshape | solution.py:53
  39.9 7.9 %broadcast_in_dim.20 = f32[2048,2048]{1,0:T(8,128)} broadcast(f32[]{:T(128)} %constant.46.clone.1), dimensions={} | broadcast | bytes 16777220 | tf_op jit(solution)/shard_map/broadcast_in_dim | solution.py:67
  47.8 17.3 %while.21 = (s32[]{:T(128)}, f32[2048,2048]{1,0:T(8,128)}, s32[]{:T(128)}, bf16[1,512,2048]{2,1,0:T(8,128)(2,1)}, bf16[1,512,2048]{2,1,0:T(8,128)(2,1)}, /*index=5*/s32[]{:T(128)}) while((s32[]{:T(128)}, f32[2048,2048]{1,0:T(8,128)}, s32[]{:T(128)}, bf16[1,512,2048]{2,1,0:T(8,128)(2,1)}, bf16[1,512,2048]{2,1,0:T(8,128)(2,1)}, ...), condition=%wide.region_5.6_spmd, body=%wide.region_4.5_spmd.sunk | while | flops 4299161600 | bytes 37748804 | solution.py:63
  47.8 17.3 %convolution_add_fusion.2 = f32[2048,2048]{1,0:T(8,128)} fusion(f32[2048,2048]{1,0:T(8,128)} %get-tuple-element.178, bf16[1,512,2048]{2,1,0:T(8,128)(2,1)} %get-tuple-element.187, bf16[1,512,2048]{2,1,0:T(8,128)(2,1)} %get-tuple-element.186), kind=kOutput, calls=%fused_computation.10.clone.1 | convolution fusion | flops 4299161600 | bytes 37748736 | tf_op jit(solution)/shard_map/while/body/dot_general | solution.py:58
  65.1 125.9 %reduce-scatter.2.cloned.1.call-done = f32[64,2048]{1,0:T(8,128)} async-done(((f32[2048,2048]{1,0:T(8,128)}), f32[64,2048]{1,0:T(8,128)}) %reduce-scatter.2.cloned.1.call-update) | async-done | bytes 524304 | tf_op jit(solution)/shard_map/reduce_scatter | solution.py:62
  191.0 1.5 collective-permute-start
  192.5 11.2 %collective-permute-done = f32[64,2048]{1,0:T(8,128)S(1)} collective-permute-done((f32[64,2048]{1,0:T(8,128)}, f32[64,2048]{1,0:T(8,128)S(1)}, u32[]{:S(2)}, u32[]{:S(2)}) %collective-permute-start) | collective-permute-done | bytes 524320 | tf_op jit(solution)/shard_map/ppermute | solution.py:82
  203.7 1.1 add.80
  204.8 2.7 collective-permute-start.1
  207.6 21.1 %collective-permute-done.1 = f32[64,2048]{1,0:T(8,128)} collective-permute-done((f32[64,2048]{1,0:T(8,128)S(1)}, f32[64,2048]{1,0:T(8,128)}, u32[]{:S(2)}, u32[]{:S(2)}) %collective-permute-start.1) | collective-permute-done | bytes 524320 | tf_op jit(solution)/shard_map/ppermute | solution.py:82
  228.8 1.1 add.81
  229.9 5.9 %collective-permute-start.2 = (f32[64,2048]{1,0:T(8,128)S(1)}, f32[64,2048]{1,0:T(8,128)S(1)}, u32[]{:S(2)}, u32[]{:S(2)}) collective-permute-start(f32[64,2048]{1,0:T(8,128)S(1)} %add.81), channel_id=1, source_target_pairs={{0,128},{32,160},{64,192},{96,224},{128,0},{160,32},{192,64},{224,... | collective-permute-start | bytes 1572872 | tf_op jit(solution)/shard_map/ppermute | solution.py:82
  235.8 7.1 %while.20 = (s32[]{:T(128)}, f32[4,32,64]{2,1,0:T(8,128)S(1)}, f32[4,32,64]{2,1,0:T(8,128)S(1)}, bf16[4,32,512]{2,1,0:T(8,128)(2,1)}, f32[64,512]{1,0:T(8,128)S(1)}, /*index=5*/s32[]{:T(128)}) while((s32[]{:T(128)}, f32[4,32,64]{2,1,0:T(8,128)S(1)}, f32[4,32,64]{2,1,0:T(8,128)S(1)}, bf16[4,32,512]{2,1,0:T(8,128)(2,1)}, ...), condition=%wide.region_2.3_spmd, body=%wide.region_0.2_spmd.sunk | while | flops 4208642 | bytes 360529 | solution.py:32
  235.8 0.8 bitcast_convert_fusion.2
  236.6 1.0 abs_reduce_fusion.2
  237.6 0.8 bitcast_convert_fusion.2
  238.4 1.0 abs_reduce_fusion.2
  239.4 0.8 bitcast_convert_fusion.2
  240.1 1.0 abs_reduce_fusion.2
  241.1 0.8 bitcast_convert_fusion.2
  241.9 1.0 abs_reduce_fusion.2
  242.9 37.9 %pmax.7 = f32[128,64]{1,0:T(8,128)S(1)} all-reduce(f32[128,64]{1,0:T(8,128)S(1)} %bitcast.35), channel_id=1, replica_groups=mesh['cont'=8,'line'=8,'scen'=4] {'cont'}, use_global_device_ids=true, to_apply=%region_3.4 | all-reduce | flops 8192 | bytes 65536 | tf_op jit(solution)/shard_map/pmax | solution.py:39
  280.9 0.7 copy.17
  281.6 0.9 add_multiply_fusion
  (27 shorter events, 0.3 us)
Async XLA Ops:
  7.2 10.2 %copy-start = (bf16[512,2048]{1,0:T(8,128)(2,1)S(1)}, bf16[512,2048]{1,0:T(8,128)(2,1)}, u32[]{:S(2)}) copy-start(bf16[512,2048]{1,0:T(8,128)(2,1)} %param.19) | copy-start | bytes 6291460
  7.2 6.8 %copy-start.2 = (bf16[128,2048]{1,0:T(8,128)(2,1)S(1)}, bf16[128,2048]{1,0:T(8,128)(2,1)}, u32[]{:S(2)}) copy-start(bf16[128,2048]{1,0:T(8,128)(2,1)} %param.18) | copy-start | bytes 1572868
  7.2 183.8 %reduce-scatter.2.cloned.1.call-start = ((), (), s32[]{:S(2)}) async-start(), calls=%async_computation.1 | async-start | bytes 17301504 | tf_op jit(solution)/shard_map/reduce_scatter | solution.py:62
  20.6 4.2 %copy-start.1 = (f32[128]{0:T(128)S(1)}, f32[128]{0:T(128)}, u32[]{:S(2)}) copy-start(f32[128]{0:T(128)} %param.17) | copy-start | bytes 1540
  24.9 3.4 %copy-start.3 = (f32[128,64]{0,1:T(8,128)S(1)}, f32[128,64]{0,1:T(8,128)}, u32[]{:S(2)}) copy-start(f32[128,64]{0,1:T(8,128)} %param.15) | copy-start | bytes 98308
  24.9 7.1 %copy-start.4 = (f32[64,512]{1,0:T(8,128)S(1)}, f32[64,512]{1,0:T(8,128)}, u32[]{:S(2)}) copy-start(f32[64,512]{1,0:T(8,128)} %param.16) | copy-start | bytes 393220
  191.0 12.7 %collective-permute-start = (f32[64,2048]{1,0:T(8,128)}, f32[64,2048]{1,0:T(8,128)S(1)}, u32[]{:S(2)}, u32[]{:S(2)}) collective-permute-start(f32[64,2048]{1,0:T(8,128)} %reduce-scatter.2.cloned.1.call-done), channel_id=1, source_target_pairs={{0,32},{32,0},{64,96},{96,64},{128,160},{160,128},{192,224},{224,1... | collective-permute-start | bytes 1572872 | tf_op jit(solution)/shard_map/ppermute | solution.py:82
  204.8 23.9 %collective-permute-start.1 = (f32[64,2048]{1,0:T(8,128)S(1)}, f32[64,2048]{1,0:T(8,128)}, u32[]{:S(2)}, u32[]{:S(2)}) collective-permute-start(f32[64,2048]{1,0:T(8,128)S(1)} %add.80), channel_id=1, source_target_pairs={{0,64},{32,96},{64,0},{96,32},{128,192},{160,224},{192,128},{224,1... | collective-permute-start | bytes 1572872 | tf_op jit(solution)/shard_map/ppermute | solution.py:82
  229.9 51.7 %collective-permute-start.2 = (f32[64,2048]{1,0:T(8,128)S(1)}, f32[64,2048]{1,0:T(8,128)S(1)}, u32[]{:S(2)}, u32[]{:S(2)}) collective-permute-start(f32[64,2048]{1,0:T(8,128)S(1)} %add.81), channel_id=1, source_target_pairs={{0,128},{32,160},{64,192},{96,224},{128,0},{160,32},{192,64},{224,... | collective-permute-start | bytes 1572872 | tf_op jit(solution)/shard_map/ppermute | solution.py:82
Sparse Core Ops, SparseCore 0:
  65.3 125.7 reduce-scatter.1
